TPU v7x, 32 devices: a whole 2x2x4 slice. The times are simulated.
32 devices in a mesh: dp: 16 (over z, y, core), tensor: 2 (over x).
Axes of the slice: x: 2, y: 2, z: 4, core: 2. Of those that a mesh axis runs over, the one named last changes fastest.
Arguments:
- layer_input: float32 [25216, 512], P('dp'), may hold values from -6 to 6
- cotangent: float32 [25216, 512], P('dp'), may hold values from -6 to 6
- ln1_gain: float32 [512], replicated, may hold values from 0.1 to 1.9
- ln1_shift: float32 [512], replicated, may hold values from -1.75 to 1.75
- w_qkv: bfloat16 [3, 512, 512], P(None, None, 'tensor'), may hold values from -0.375 to 0.375
- qv_bias: float32 [2, 512], P(None, 'tensor'), may hold values from -3 to 3
- w_out: bfloat16 [512, 512], P('tensor'), may hold values from -0.75 to 0.75
- out_bias: float32 [512], replicated, may hold values from -1.75 to 1.75
- ln2_gain: float32 [512], replicated, may hold values from 0.1 to 1.9
- ln2_shift: float32 [512], replicated, may hold values from -1.75 to 1.75
- w_router: float32 [512, 4], replicated, may hold values from -0.125 to 0.125
- w_in: bfloat16 [4, 512, 2048], P(None, None, 'tensor'), may hold values from -0.25 to 0.25
- in_bias: float32 [4, 2048], P(None, 'tensor'), may hold values from -1.75 to 1.75
- w_hidden_out: bfloat16 [4, 2048, 512], P(None, 'tensor'), may hold values from -0.5 to 0.5
- choices: int32 [25216, 2], P('dp'), may hold values from 0 to 3, as said below
- priority: int32 [16, 1576], P('dp'), may hold values from 0 to 1575, each once within a row
Outputs:
- layer_out: float32 [25216, 512], P('dp')
- input_grad: float32 [25216, 512], P('dp')
- ln1_gain_grad: float32 [512], replicated
- ln1_shift_grad: float32 [512], replicated
- w_qkv_grad: float32 [3, 512, 512], P(None, None, 'tensor')
- qv_bias_grad: float32 [2, 512], P(None, 'tensor')
- w_out_grad: float32 [512, 512], P('tensor')
- out_bias_grad: float32 [512], replicated
- ln2_gain_grad: float32 [512], replicated
- ln2_shift_grad: float32 [512], replicated
- w_router_grad: float32 [512, 4], replicated
- w_in_grad: float32 [4, 512, 2048], P(None, None, 'tensor')
- in_bias_grad: float32 [4, 2048], P(None, 'tensor')
- w_hidden_out_grad: float32 [4, 2048, 512], P(None, 'tensor')
Inputs may be any that keep to these rules, and one draw needn't show every extreme that they name: `choices`: each row names two different experts; every expert is named by some row. `priority`: each row is a permutation of 0 to 1575 giving the dispatch rank of the tokens of one data shard, lower first.
All inputs are finite; a program needn't handle non-finite values.
Results may differ from a plain program's by a relative error of at most 0.013.
The roundings to bfloat16 on the way count: a program that leaves them out, or rounds other values in their place, can miss the bound.
Values sent between devices are 32-bit elements; how exact they have to be, the bound alone decides.
A program may use at most 192 MiB of HBM per device.

v0:
```python
import jax
import jax.numpy as jnp
from jax import lax
from jax.sharding import PartitionSpec as P

HEAD_DIM = 64
SEQ = 197


epsilon = 1e-06
HIGHEST = lax.Precision.HIGHEST


def layer_norm(inputs, ln_gain, ln_shift):
    row_mean = jnp.mean(inputs, axis=-1, keepdims=True)
    centred = inputs - row_mean
    row_var = jnp.mean(centred * centred, axis=-1, keepdims=True)
    return centred * lax.rsqrt(row_var + epsilon) * ln_gain + ln_shift


def softmax_rows(scores):
    row_max = jnp.max(scores, axis=-1, keepdims=True)
    exp_rows = jnp.exp(scores - row_max)
    return exp_rows / jnp.sum(exp_rows, axis=-1, keepdims=True)


def gelu_tanh(pre_vals):
    return jax.nn.gelu(pre_vals, approximate=True)


def slot_table(choices, priority, experts_n, capacity):
    tok_count = choices.shape[0]
    token_ids = jnp.arange(tok_count, dtype=jnp.int32)
    ranked_ids = jnp.zeros((tok_count,), jnp.int32).at[priority].set(token_ids)
    ranked_choice = choices[ranked_ids]
    onehot = (
        ranked_choice.T[:, :, None] == jnp.arange(experts_n, dtype=jnp.int32)[None, None, :]
    ).astype(jnp.int32)
    flat_hits = onehot.reshape(2 * tok_count, experts_n)
    earlier = jnp.cumsum(flat_hits, axis=0) - flat_hits
    position = jnp.sum(earlier * flat_hits, axis=1).reshape(2, tok_count)
    position = position[:, priority].T
    kept_mask = position < capacity
    slot_ids = jnp.where(kept_mask, choices * capacity + position, experts_n * capacity)
    pair_token = jnp.broadcast_to(token_ids[:, None], (tok_count, 2))
    slot_token = (
        jnp.full((experts_n * capacity + 1,), tok_count, jnp.int32)
        .at[slot_ids.reshape(-1)]
        .set(pair_token.reshape(-1))
    )
    return (slot_ids, kept_mask, slot_token[: experts_n * capacity])


def local(
    layer_input,
    cotangent,
    ln1_gain,
    ln1_shift,
    w_qkv,
    qv_bias,
    w_out,
    out_bias,
    ln2_gain,
    ln2_shift,
    w_router,
    w_in,
    in_bias,
    w_hidden_out,
    choices,
    priority,
):
    tok_count = layer_input.shape[0]
    model_width = layer_input.shape[1]
    experts_n = w_in.shape[0]
    capacity = (5 * tok_count + 2 * experts_n - 1) // (2 * experts_n)
    local_heads = w_qkv.shape[2] // HEAD_DIM
    flat_width = local_heads * HEAD_DIM
    head_shape = (tok_count // SEQ, SEQ, local_heads, HEAD_DIM)
    score_scale = HEAD_DIM ** (-0.5)
    slot_ids, kept_mask, slot_token = slot_table(choices, priority[0], experts_n, capacity)
    normed, pull_norm_one = jax.vjp(layer_norm, layer_input, ln1_gain, ln1_shift)
    normed_low = normed.astype(jnp.bfloat16)
    projected = jnp.einsum("td,jdf->jtf", normed_low, w_qkv, preferred_element_type=jnp.float32)
    queries = (projected[0] + qv_bias[0]).astype(jnp.bfloat16).reshape(head_shape)
    key_rows = projected[1].astype(jnp.bfloat16).reshape(head_shape)
    value_rows = (projected[2] + qv_bias[1]).astype(jnp.bfloat16).reshape(head_shape)
    scores = (
        jnp.einsum("bqhd,bkhd->bhqk", queries, key_rows, preferred_element_type=jnp.float32)
        * score_scale
    )
    row_max = jnp.max(scores, axis=-1, keepdims=True)
    exp_rows = jnp.exp(scores - row_max)
    row_sum = jnp.sum(exp_rows, axis=-1, keepdims=True)
    log_total = row_max + jnp.log(row_sum)
    softmaxed = (exp_rows / row_sum).astype(jnp.bfloat16)
    attended = jnp.einsum(
        "bhqk,bkhd->bqhd", softmaxed, value_rows, preferred_element_type=jnp.float32
    )
    attended = attended.reshape(tok_count, flat_width).astype(jnp.bfloat16)
    partial_branch = jnp.dot(attended, w_out, preferred_element_type=jnp.float32)
    middle = layer_input + lax.psum(partial_branch, "tensor") + out_bias
    normed_two, pull_norm_two = jax.vjp(layer_norm, middle, ln2_gain, ln2_shift)
    routed_in = normed_two.astype(jnp.bfloat16)

    def route(rows_in, table):
        router = softmax_rows(jnp.dot(rows_in, table, precision=HIGHEST))
        return jnp.take_along_axis(router, choices, axis=1)

    gates, pull_route = jax.vjp(route, routed_in.astype(jnp.float32), w_router)
    padded = jnp.concatenate([routed_in, jnp.zeros((1, model_width), jnp.bfloat16)], axis=0)
    expert_in = padded[slot_token].reshape(experts_n, capacity, model_width)
    pre_act = (
        jnp.einsum("ecd,edf->ecf", expert_in, w_in, preferred_element_type=jnp.float32)
        + in_bias[:, None, :]
    )
    activated, pull_gelu = jax.vjp(gelu_tanh, pre_act)
    hidden = activated.astype(jnp.bfloat16)
    partial_out = jnp.einsum(
        "ecf,efd->ecd", hidden, w_hidden_out, preferred_element_type=jnp.float32
    )
    out_pad = jnp.concatenate(
        [
            partial_out.reshape(experts_n * capacity, model_width),
            jnp.zeros((1, model_width), jnp.float32),
        ],
        axis=0,
    )
    pair_weight = jnp.where(
        kept_mask, gates.astype(jnp.bfloat16).astype(jnp.float32), jnp.float32(0.0)
    )
    rows_first = out_pad[slot_ids[:, 0]]
    rows_second = out_pad[slot_ids[:, 1]]
    partial_comb = pair_weight[:, 0:1] * rows_first + pair_weight[:, 1:2] * rows_second
    partial_gate = jnp.stack(
        [jnp.sum(cotangent * rows_first, axis=1), jnp.sum(cotangent * rows_second, axis=1)], axis=1
    )
    combined, gate_total = lax.psum((partial_comb, partial_gate), "tensor")
    layer_out = middle + combined
    gate_grad = jnp.where(kept_mask, gate_total, jnp.float32(0.0))
    slot_weight = (
        jnp.zeros((experts_n * capacity + 1,), jnp.float32)
        .at[slot_ids.reshape(-1)]
        .set(pair_weight.reshape(-1))[: experts_n * capacity]
    )
    cot_pad = jnp.concatenate([cotangent, jnp.zeros((1, model_width), jnp.float32)], axis=0)
    out_grad = (
        (slot_weight[:, None] * cot_pad[slot_token])
        .astype(jnp.bfloat16)
        .reshape(experts_n, capacity, model_width)
    )
    routed_grad, router_grad = pull_route(gate_grad)
    hidden_grad = jnp.einsum(
        "ecd,efd->ecf", out_grad, w_hidden_out, preferred_element_type=jnp.float32
    )
    w_hidden_out_grad = jnp.einsum(
        "ecf,ecd->efd", hidden, out_grad, preferred_element_type=jnp.float32
    )
    pre_grad = pull_gelu(hidden_grad)[0].astype(jnp.bfloat16)
    in_bias_grad = jnp.sum(pre_grad.astype(jnp.float32), axis=1)
    w_in_grad = jnp.einsum("ecd,ecf->edf", expert_in, pre_grad, preferred_element_type=jnp.float32)
    input_rows_grad = jnp.einsum(
        "ecf,edf->ecd", pre_grad, w_in, preferred_element_type=jnp.float32
    ).reshape(experts_n * capacity, model_width)
    grad_pad = jnp.concatenate([input_rows_grad, jnp.zeros((1, model_width), jnp.float32)], axis=0)
    partial_routed = grad_pad[slot_ids[:, 0]] + grad_pad[slot_ids[:, 1]]
    routed_total = lax.psum(partial_routed, "tensor") + routed_grad
    middle_ln, ln2_gain_grad, ln2_shift_grad = pull_norm_two(routed_total)
    middle_grad = cotangent + middle_ln
    router_grad, w_in_grad, in_bias_grad, w_hidden_out_grad = lax.psum(
        (router_grad, w_in_grad, in_bias_grad, w_hidden_out_grad), "dp"
    )
    branch_grad = middle_grad.astype(jnp.bfloat16)
    out_bias_grad = jnp.sum(branch_grad.astype(jnp.float32), axis=0)
    w_out_grad = jnp.einsum("tf,td->fd", attended, branch_grad, preferred_element_type=jnp.float32)
    attended_grad = (
        jnp.einsum("td,fd->tf", branch_grad, w_out, preferred_element_type=jnp.float32)
        .astype(jnp.bfloat16)
        .reshape(head_shape)
    )
    scores_again = (
        jnp.einsum("bqhd,bkhd->bhqk", queries, key_rows, preferred_element_type=jnp.float32)
        * score_scale
    )
    probs_again = jnp.exp(scores_again - log_total)
    probs_grad = jnp.einsum(
        "bqhd,bkhd->bhqk", attended_grad, value_rows, preferred_element_type=jnp.float32
    )
    value_grad = jnp.einsum(
        "bhqk,bqhd->bkhd", softmaxed, attended_grad, preferred_element_type=jnp.float32
    ).astype(jnp.bfloat16)
    scores_grad = (
        probs_again * (probs_grad - jnp.sum(probs_grad * probs_again, axis=-1, keepdims=True))
    ).astype(jnp.bfloat16)
    query_grad = (
        jnp.einsum("bhqk,bkhd->bqhd", scores_grad, key_rows, preferred_element_type=jnp.float32)
        * score_scale
    ).astype(jnp.bfloat16)
    key_grad = (
        jnp.einsum("bhqk,bqhd->bkhd", scores_grad, queries, preferred_element_type=jnp.float32)
        * score_scale
    ).astype(jnp.bfloat16)
    query_flat = query_grad.reshape(tok_count, flat_width)
    value_flat = value_grad.reshape(tok_count, flat_width)
    proj_grad = jnp.stack([query_flat, key_grad.reshape(tok_count, flat_width), value_flat], axis=0)
    w_qkv_grad = jnp.einsum(
        "td,jtf->jdf", normed_low, proj_grad, preferred_element_type=jnp.float32
    )
    qv_bias_grad = jnp.stack(
        [
            jnp.sum(query_flat.astype(jnp.float32), axis=0),
            jnp.sum(value_flat.astype(jnp.float32), axis=0),
        ],
        axis=0,
    )
    partial_normed = jnp.einsum("jtf,jdf->td", proj_grad, w_qkv, preferred_element_type=jnp.float32)
    normed_grad = lax.psum(partial_normed, "tensor")
    input_ln, ln1_gain_grad, ln1_shift_grad = pull_norm_one(normed_grad)
    input_grad = middle_grad + input_ln
    (
        ln1_gain_grad,
        ln1_shift_grad,
        w_qkv_grad,
        qv_bias_grad,
        w_out_grad,
        out_bias_grad,
        ln2_gain_grad,
        ln2_shift_grad,
    ) = lax.psum(
        (
            ln1_gain_grad,
            ln1_shift_grad,
            w_qkv_grad,
            qv_bias_grad,
            w_out_grad,
            out_bias_grad,
            ln2_gain_grad,
            ln2_shift_grad,
        ),
        "dp",
    )
    return (
        layer_out,
        input_grad,
        ln1_gain_grad,
        ln1_shift_grad,
        w_qkv_grad,
        qv_bias_grad,
        w_out_grad,
        out_bias_grad,
        ln2_gain_grad,
        ln2_shift_grad,
        router_grad,
        w_in_grad,
        in_bias_grad,
        w_hidden_out_grad,
    )


def solution(mesh):
    placed = (
        P("dp", None),
        P("dp", None),
        P(),
        P(),
        P(None, None, "tensor"),
        P(None, "tensor"),
        P("tensor", None),
        P(),
        P(),
        P(),
        P(),
        P(None, None, "tensor"),
        P(None, "tensor"),
        P(None, "tensor", None),
        P("dp", None),
        P("dp", None),
    )
    return jax.shard_map(
        local,
        mesh=mesh,
        in_specs=placed,
        out_specs=(
            P("dp", None),
            P("dp", None),
            P(),
            P(),
            P(None, None, "tensor"),
            P(None, "tensor"),
            P("tensor", None),
            P(),
            P(),
            P(),
            P(),
            P(None, None, "tensor"),
            P(None, "tensor"),
            P(None, "tensor", None),
        ),
        check_vma=False,
    )
```

profile of v0, /device:TPU:3, one launch (start us, length us, event | category | flops | bytes accessed | tf_op | source)
XLA Modules:
  0.0 969.5 jit_solution(12831830087404362826)
XLA Ops:
  7.3 2.3 reduce_sum.218
  9.6 2.6 multiply_reduce_fusion.9
  17.6 2.3 copy.169
  19.9 2.9 squeeze.6
  22.7 2.8 reshape.383
  26.6 2.1 copy.170
  28.8 2.9 squeeze.7
  31.7 1.9 add_convert_fusion.2
  43.1 2.3 fusion.58
  46.1 9.0 scatter_custom_fusion
  55.4 3.2 gather_fusion
  62.0 3.2 gather_fusion.1
  68.4 3.9 concatenate.14
  72.3 15.8 %scatter_custom_fusion.1 = s32[3941]{0:T(1024)S(1)} fusion(s32[3152]{0:T(1024)S(1)} %fusion.33, s32[3152]{0:T(1024)S(1)} %reshape.357, s32[]{:T(128)} %constant.29.clone.1), kind=kCustom, calls=%fused_computation.132 | custom fusion | bytes 15768 | tf_op jit(solution)/shard_map/scatter | solution.py:49
  88.2 15.2 %gather_fusion.5 = f32[3940,512]{1,0:T(8,128)} fusion(f32[1577,512]{1,0:T(8,128)} %concatenate.14, s32[4096]{0:T(1024)S(1)} %pad_clamp_fusion), kind=kCustom, calls=%fused_computation.5 | custom fusion | bytes 16154000 | tf_op jit(solution)/shard_map/gather | solution.py:147
  103.5 7.5 gather.37
  112.2 21.1 %all-reduce.13.cloned.1.call-done = f32[1576,512]{1,0:T(8,128)} async-done(((f32[1576,512]{1,0:T(8,128)}), f32[1576,512]{1,0:T(8,128)}) %all-reduce.13.cloned.1.call-update) | async-done | bytes 3227664 | tf_op jit(solution)/shard_map/psum | solution.py:101
  133.3 3.3 fusion.55
  140.4 38.6 %gather_fusion.8 = bf16[3152]{0:T(1024)(128)(2,1)S(1)} fusion(bf16[1576,4]{0,1:T(4,128)(2,1)S(1)} %broadcast_divide_fusion, s32[3152]{0:T(1024)S(1)} %reshape.339), kind=kCustom, calls=%fused_computation.8 | custom fusion | bytes 37824 | tf_op jit(solution)/shard_map/jvp(jit(take_along_axis))/gather | solution.py:107
  180.8 15.8 %scatter_custom_fusion.2 = f32[3941]{0:T(1024)S(1)} fusion(s32[3152]{0:T(1024)S(1)} %fusion.33, f32[3152]{0:T(1024)S(1)} %reshape.365, f32[]{:T(128)} %constant.23.clone.1), kind=kCustom, calls=%fused_computation.130 | custom fusion | bytes 15768 | tf_op jit(solution)/shard_map/scatter | solution.py:143
  198.3 12.8 %gather_fusion.2 = bf16[3940,512]{1,0:T(8,128)(2,1)} fusion(bf16[1577,512]{1,0:T(8,128)(2,1)S(1)} %concatenate.12, s32[4096]{0:T(1024)S(1)} %pad_clamp_fusion), kind=kCustom, calls=%fused_computation.2 | custom fusion | bytes 8084880 | tf_op jit(solution)/shard_map/gather | solution.py:111
  211.0 5.2 reshape.265
  216.3 15.0 %multiply_convert_fusion = (bf16[4,985,1024]{2,1,0:T(8,128)(2,1)}, f32[4,985,1024]{2,1,0:T(8,128)}) fusion(f32[4,1024]{1,0:T(4,128)S(1)} %copy-done.66, bf16[4,985,512]{2,1,0:T(8,128)(2,1)} %reshape.265, bf16[4,512,1024]{2,1,0:T(8,128)(2,1)} %param.27), kind=kOutput, calls=%fused_computation.23 | convolution fusion | flops 4171735040 | bytes 32452608 | tf_op jit(solution)/shard_map/ecd,edf->ecf/dot_general | solution.py:113
  231.3 19.6 %convert_reduce_fusion = (f32[4,1024]{1,0:T(4,128)S(1)}, bf16[4,985,1024]{2,1,0:T(8,128)(2,1)}) fusion(f32[4,985,1024]{2,1,0:T(8,128)} %get-tuple-element.133, f32[4,1024]{1,0:T(4,128)S(1)} %copy-done.66, bf16[4,1024,512]{2,1,0:T(8,128)(2,1)S(1)} %copy-done.65, f32[4,985,512]{2,1,0:T(8,128)} %gather.37, f32[4,985]{1,0:T(4,128)S(1)} %mul.259), kind=kOutput, calls=%fused_computation.22 | convolution fusion | flops 4228214784 | bytes 36519312 | tf_op jit(solution)/shard_map/ecd,efd->ecf/dot_general | solution.py:152
  250.9 10.1 %fusion.60 = f32[4,985,512]{2,1,0:T(8,128)} fusion(bf16[4,985,1024]{2,1,0:T(8,128)(2,1)} %get-tuple-element.144, bf16[4,512,1024]{2,1,0:T(8,128)(2,1)S(1)} %copy-done.64), kind=kOutput, calls=%fused_computation.168 | convolution fusion | flops 4131389440 | bytes 20332544 | tf_op jit(solution)/shard_map/ecf,edf->ecd/dot_general | solution.py:161
  261.0 7.6 reshape.268
  268.6 7.6 concatenate.15
  276.2 9.6 gather_fusion.7
  285.8 9.6 gather_fusion.6
  295.4 5.3 add.234
  300.8 12.2 %fusion.59 = f32[4,985,512]{2,1,0:T(8,128)} fusion(bf16[4,985,1024]{2,1,0:T(8,128)(2,1)} %get-tuple-element.132, bf16[4,1024,512]{2,1,0:T(8,128)(2,1)} %param.29), kind=kOutput, calls=%fused_computation.167 | convolution fusion | flops 4131389440 | bytes 20332544 | tf_op jit(solution)/shard_map/ecf,efd->ecd/dot_general | solution.py:118
  313.0 7.6 reshape.266
  320.6 7.6 concatenate.13
  328.2 9.8 %gather_fusion.4 = f32[1576,512]{1,0:T(8,128)} fusion(f32[3941,512]{1,0:T(8,128)} %concatenate.13, s32[2048]{0:T(1024)S(1)} %copy-done.51), kind=kCustom, calls=%fused_computation.4 | custom fusion | bytes 6461600 | tf_op jit(solution)/shard_map/gather | solution.py:132
  338.0 9.6 gather_fusion.3
  347.7 6.7 multiply_reduce_fusion.7
  354.4 7.6 psum.122
  362.7 18.2 %scatter_custom_fusion.3 = f32[6304]{0:T(1024)S(1)} fusion(s32[3152]{0:T(1024)} %reshape.369, f32[3152]{0:T(1024)S(1)} %reshape.371, f32[]{:T(128)} %constant.23.clone.1), kind=kCustom, calls=%fused_computation.106 | custom fusion | flops 3152 | bytes 25728
  381.2 7.6 all-reduce.15.cloned.1.call-done
  388.8 7.3 multiply_reduce_fusion.2
  401.8 3.1 copy.191
  405.0 4.2 convert_reduce_fusion.2
  409.1 7.6 multiply_reduce_fusion
  416.8 4.7 multiply_convert_fusion.2
  421.5 2.1 fusion.14
  425.4 2.3 copy.212
  427.7 3.7 reshape.382
  431.5 3.9 copy.211
  435.4 3.6 reshape.381
  439.0 2.3 copy.210
  441.4 3.7 reshape.380
  447.6 3.1 convolution_bitcast_fusion.1
  450.9 12.5 %fusion.62 = f32[4,512,1024]{2,1,0:T(8,128)} fusion(bf16[4,985,512]{2,1,0:T(8,128)(2,1)} %reshape.265, bf16[4,985,1024]{2,1,0:T(8,128)(2,1)} %get-tuple-element.144), kind=kOutput, calls=%fused_computation.170 | convolution fusion | flops 4131389440 | bytes 20492288 | tf_op jit(solution)/shard_map/ecd,ecf->edf/dot_general | solution.py:160
  463.4 14.2 %fusion.9 = f32[4,1024,512]{2,1,0:T(8,128)} fusion(bf16[4,985,1024]{2,1,0:T(8,128)(2,1)} %get-tuple-element.132, f32[4,985,512]{2,1,0:T(8,128)} %gather.37, f32[4,985]{1,0:T(4,128)S(1)} %mul.259), kind=kOutput, calls=%fused_computation.61 | convolution fusion | flops 4135424000 | bytes 24542608 | tf_op jit(solution)/shard_map/ecf,ecd->efd/dot_general | solution.py:155
  479.1 5.5 convolution_bitcast_fusion.2
  487.0 120.9 %all-reduce.19.cloned.1.call-done = (f32[1576,512]{1,0:T(8,128)}, f32[1576,512]{1,0:T(8,128)}) async-done(((f32[1576,512]{1,0:T(8,128)}, f32[1576,512]{1,0:T(8,128)}), (f32[1576,512]{1,0:T(8,128)}, f32[1576,512]{1,0:T(8,128)})) %all-reduce.19.cloned.1.call-update) | async-done | bytes 6455312 | tf_op jit(solution)/shard_map/psum | solution.py:137
  608.0 5.7 add.233
  614.9 60.7 %all-reduce.5 = (f32[512]{0:T(512)}, f32[512]{0:T(512)}, f32[2,256]{1,0:T(2,128)}, f32[512]{0:T(512)}, f32[512]{0:T(512)}, /*index=5*/f32[512]{0:T(512)}, f32[512,4]{0,1:T(4,128)}, f32[4,1024]{1,0:T(4,128)}) all-reduce(f32[512]{0:T(512)S(1)} %get-tuple-element.86, ...), channel_id=1, replica_groups=mesh['dp'=16,'tensor'=2] {'dp'}, use_global_device_ids=true, to_apply=%region_31.32 | all-reduce | flops 9216 | bytes 73728 | tf_op jit(solution)/shard_map/psum | solution.py:228
  675.6 4.6 fusion.52
  681.1 2.2 add_add_fusion.2
  683.3 263.2 %all-reduce.17.cloned.1.call-done = (f32[3,512,256]{1,2,0:T(8,128)}, f32[256,512]{1,0:T(8,128)}, f32[4,512,1024]{2,1,0:T(8,128)}, f32[4,1024,512]{2,1,0:T(8,128)}) async-done(((f32[3,512,256]{1,2,0:T(8,128)}, f32[256,512]{1,0:T(8,128)}, f32[4,512,1024]{2,1,0:T(8,128)}, f32[4,1024,512]{2,1,0:T(8,128)}), (f32[3,512,256]{1,2,0:T(8,128)}, f32[256,512]{1,0:T(8,128)}, f32[4,512,1024]{2,1,0:T(8,128)}, ...) | async-done | bytes 18874384 | tf_op jit(solution)/shard_map/psum | solution.py:228
  946.4 3.1 copy.205
  950.3 9.0 copy.246
  959.3 3.4 copy.247
  (260 shorter events, 49.6 us)
Async XLA Ops:
  7.2 5.6 copy-start
  7.2 5.6 copy-start.56
  7.2 5.6 copy-start.67
  7.2 126.1 %all-reduce.13.cloned.1.call-start = ((), (), s32[]{:S(2)}) async-start(), calls=%async_computation | async-start | bytes 6455296 | tf_op jit(solution)/shard_map/psum | solution.py:101
  9.5 3.3 copy-start.4
  9.6 5.0 copy-start.40
  12.9 1.7 copy-start.48
  15.5 1.9 copy-start.61
  26.6 7.0 copy-start.16
  34.9 2.8 copy-start.1
  39.2 1.6 copy-start.8
  39.5 1.6 copy-start.20
  41.2 1.9 copy-start.26
  43.0 2.3 copy-start.14
  45.4 9.7 %copy-start.33 = (s32[1576,2]{0,1:T(2,128)S(1)}, s32[1576,2]{0,1:T(2,128)}, u32[]{:S(2)}) copy-start(s32[1576,2]{0,1:T(2,128)} %param.30) | copy-start | bytes 37828
  45.4 343.4 %all-reduce.15.cloned.1.call-start = ((), (), s32[]{:S(2)}) async-start(), calls=%async_computation.1 | async-start | bytes 6455296 | tf_op jit(solution)/shard_map/psum | solution.py:166
  58.6 7.8 copy-start.63
  58.9 7.6 copy-start.62
  103.5 29.9 %copy-start.59 = (f32[512]{0:T(512)S(1)}, f32[512]{0:T(512)}, u32[]{:S(2)}) copy-start(f32[512]{0:T(512)} %param.23) | copy-start | bytes 6148
  136.7 1.7 copy-start.2
  137.4 2.3 copy-start.46
  137.7 2.1 copy-start.42
  140.4 38.7 %copy-start.38 = (f32[1576]{0:T(1024)}, f32[1576]{0:T(1024)S(1)}, u32[]{:S(2)}) copy-start(f32[1576]{0:T(1024)S(1)} %fusion.48) | copy-start | bytes 18916
  211.0 5.2 copy-start.66
  216.3 15.0 %copy-start.65 = (bf16[4,1024,512]{2,1,0:T(8,128)(2,1)S(1)}, bf16[4,1024,512]{2,1,0:T(8,128)(2,1)}, u32[]{:S(2)}) copy-start(bf16[4,1024,512]{2,1,0:T(8,128)(2,1)} %param.29) | copy-start | bytes 12582916
  231.3 19.6 %copy-start.64 = (bf16[4,512,1024]{2,1,0:T(8,128)(2,1)S(1)}, bf16[4,512,1024]{2,1,0:T(8,128)(2,1)}, u32[]{:S(2)}) copy-start(bf16[4,512,1024]{2,1,0:T(8,128)(2,1)} %param.27) | copy-start | bytes 12582916
  268.6 7.6 copy-start.51
  276.2 9.6 copy-start.50
  300.7 307.2 %all-reduce.19.cloned.1.call-start = ((), (), s32[]{:S(2)}) async-start(), calls=%async_computation.3 | async-start | bytes 12910592 | tf_op jit(solution)/shard_map/psum | solution.py:137
  347.7 33.3 %copy-start.39 = (f32[1576]{0:T(1024)S(1)}, f32[1576]{0:T(1024)}, u32[]{:S(2)}) copy-start(f32[1576]{0:T(1024)} %copy-done.38) | copy-start | bytes 18916
  347.7 33.4 %copy-start.29 = (f32[1576,4]{0,1:T(4,128)S(1)}, f32[1576,4]{0,1:T(4,128)}, u32[]{:S(2)}) copy-start(f32[1576,4]{0,1:T(4,128)} %copy-done.28) | copy-start | bytes 75652
  347.7 33.4 %copy-start.35 = (f32[1576]{0:T(1024)S(1)}, f32[1576]{0:T(1024)}, u32[]{:S(2)}) copy-start(f32[1576]{0:T(1024)} %copy-done.34) | copy-start | bytes 18916
  347.7 41.1 %copy-start.37 = (f32[1576]{0:T(1024)S(1)}, f32[1576]{0:T(1024)}, u32[]{:S(2)}) copy-start(f32[1576]{0:T(1024)} %copy-done.36) | copy-start | bytes 18916
  347.7 41.1 %copy-start.43 = (f32[1576]{0:T(1024)S(1)}, f32[1576]{0:T(1024)}, u32[]{:S(2)}) copy-start(f32[1576]{0:T(1024)} %copy-done.42) | copy-start | bytes 18916
  347.7 41.1 %copy-start.53 = (f32[512,4]{0,1:T(4,128)S(1)}, f32[512,4]{0,1:T(4,128)}, u32[]{:S(2)}) copy-start(f32[512,4]{0,1:T(4,128)} %param.26) | copy-start | bytes 24580
  347.7 41.1 %copy-start.55 = (f32[512]{0:T(512)S(1)}, f32[512]{0:T(512)}, u32[]{:S(2)}) copy-start(f32[512]{0:T(512)} %param.24) | copy-start | bytes 6148
  388.8 7.3 copy-start.47
  388.8 7.3 copy-start.3
  396.1 1.9 copy-start.6
  397.6 1.8 copy-start.9
  404.9 4.2 copy-start.21
  404.9 4.2 copy-start.31
  409.1 7.7 slice-start
  409.1 7.6 slice-start.1
  416.8 4.7 copy-start.19
  421.5 2.1 copy-start.17
  423.7 1.7 copy-start.23
  427.7 11.3 %copy-start.24 = (bf16[8,197,4,64]{1,3,2,0:T(8,128)(2,1)S(1)}, bf16[8,197,4,64]{1,3,2,0:T(8,128)(2,1)}, u32[]{:S(2)}) copy-start(bf16[8,197,4,64]{1,3,2,0:T(8,128)(2,1)} %get-tuple-element.142) | copy-start | bytes 2420740
  441.4 6.1 copy-start.25
  447.6 3.1 copy-start.32
  450.7 495.7 %all-reduce.17.cloned.1.call-start = ((), (), s32[]{:S(2)}) async-start(), calls=%async_computation.2 | async-start | bytes 37748736 | tf_op jit(solution)/shard_map/psum | solution.py:228
  463.4 14.2 %copy-start.15 = (bf16[1576,256]{0,1:T(8,128)(2,1)S(1)}, bf16[1576,256]{0,1:T(8,128)(2,1)}, u32[]{:S(2)}) copy-start(bf16[1576,256]{0,1:T(8,128)(2,1)} %copy-done.14) | copy-start | bytes 2420740
  463.4 15.6 %copy-start.41 = (f32[1576]{0:T(1024)S(1)}, f32[1576]{0:T(1024)}, u32[]{:S(2)}) copy-start(f32[1576]{0:T(1024)} %copy-done.40) | copy-start | bytes 18916
  463.4 15.6 %copy-start.49 = (f32[1576]{0:T(1024)S(1)}, f32[1576]{0:T(1024)}, u32[]{:S(2)}) copy-start(f32[1576]{0:T(1024)} %copy-done.48) | copy-start | bytes 18916
  463.4 15.6 %copy-start.57 = (f32[512]{0:T(512)S(1)}, f32[512]{0:T(512)}, u32[]{:S(2)}) copy-start(f32[512]{0:T(512)} %param.18) | copy-start | bytes 6148
  463.4 15.6 %copy-start.68 = (f32[512]{0:T(512)S(1)}, f32[512]{0:T(512)}, u32[]{:S(2)}) copy-start(f32[512]{0:T(512)} %param.19) | copy-start | bytes 6148
  608.0 5.7 copy-start.5
  608.0 5.7 copy-start.13
  613.7 61.9 %copy-start.45 = (f32[1576]{0:T(1024)S(1)}, f32[1576]{0:T(1024)}, u32[]{:S(2)}) copy-start(f32[1576]{0:T(1024)} %copy-done.44) | copy-start | bytes 18916
  675.6 4.6 copy-start.7
  675.6 5.5 copy-start.10
  946.4 3.1 copy-start.30
  949.5 9.8 %slice-start.2 = ((s8[8388608]{0:T(1024)(128)(4,1)}), s8[4194304]{0:T(1024)(128)(4,1)S(1)}, s32[]{:S(2)}) async-start(s8[8388608]{0:T(1024)(128)(4,1)} %bitcast.92), calls=%async_computation.6 | async-start | bytes 8388608
  950.3 9.0 slice-start.3
  (13 other events, 13.4 us)
Sparse Core Ops, SparseCore 0:
  45.5 87.7 all-reduce.12
  300.9 87.8 all-reduce.14
  450.8 157.0 all-reduce.18
  613.5 332.8 all-reduce.16
where the time goes:
time: 975 us; the launch traced here: 969 us
  waiting for transfers between devices  413 us (42%)
  local copies, waits for them, and re-layouts  279 us (29%)
  matrix products  125 us (13%)
  other arithmetic  68.6 us (7%)
  blocking collectives  68.2 us (7%)
  between operations  15.1 us (2%)
    psum x1, waiting for transfers between devices, local(): lax.psum((ln1_gain_grad, ln1_shift_grad, w_qkv_grad, qv_bias_grad, w_out_...  263 us
    psum x1, waiting for transfers between devices, local(): combined, gate_total = lax.psum((partial_comb, partial_gate), 'tensor')  121 us
    psum x1, blocking collectives, local(): lax.psum((ln1_gain_grad, ln1_shift_grad, w_qkv_grad, qv_bias_grad, w_out_...  60.7 us
    gather x7, local copies, waits for them, and re-layouts, route(): return jnp.take_along_axis(router, choices, axis=1)  40.4 us
    unnamed x156, local copies, waits for them, and re-layouts  28.9 us
    gather x2, local copies, waits for them, and re-layouts, local(): cot_pad[slot_token]  22.7 us
    psum x1, waiting for transfers between devices, local(): middle = layer_input + lax.psum(partial_branch, 'tensor') + out_bias  21.1 us
    another operation x7, local copies, waits for them, and re-layouts, local(): jnp.stack([query_flat, key_grad.reshape(tok_count, flat_width), value_fla...  19.8 us
  transfers between devices with their start and end apart: 4, of which 4 were waited for; matrix products, arithmetic and copies ran while one was open for 19% of the time, Pallas kernels for 0%

commit v1 on v0

v1 whole, which is shorter than its diff:
```python
import functools

import jax
import jax.numpy as jnp
from jax import lax
from jax.experimental import pallas as pl
from jax.experimental.pallas import tpu as pltpu
from jax.sharding import PartitionSpec as P

HEAD_DIM = 64
SEQ = 197
PAD = 208
SENT = 200
LANES = 128
EPS = 1e-06
SCALE = HEAD_DIM ** (-0.5)
BF = jnp.bfloat16
F32 = jnp.float32
MESH = pl.DeviceIdType.MESH
MIB = 1 << 20

UNITS = 18
ENTRIES = 20
SLOTS = 4
FINALS = 8
FIRST_ATT = 16
SMALL = 24


def dot(a, b):
    return jnp.dot(a, b, preferred_element_type=F32)


def dot_nt(a, b):
    return lax.dot_general(a, b, (((1,), (1,)), ((), ())), preferred_element_type=F32)


def dot_tn(a, b):
    return lax.dot_general(a, b, (((0,), (0,)), ((), ())), preferred_element_type=F32)


def rows(i, size):
    return pl.ds(pl.multiple_of(i * size, size), size)


def span(start, size):
    return pl.ds(pl.multiple_of(start, 32), size)


def iota(shape, axis):
    return lax.broadcasted_iota(jnp.int32, shape, axis)


def column(vals, index):
    return jnp.sum(jnp.where(iota(vals.shape, 1) == index, vals, 0.0), axis=1, keepdims=True)


def norm_stats(vals):
    centred = vals - jnp.mean(vals, axis=1, keepdims=True)
    inv = lax.rsqrt(jnp.mean(centred * centred, axis=1, keepdims=True) + EPS)
    return centred * inv, inv


def norm_back(grad, gain, unit, inv):
    scaled = grad * gain
    mean_one = jnp.mean(scaled, axis=1, keepdims=True)
    mean_two = jnp.mean(scaled * unit, axis=1, keepdims=True)
    return inv * (scaled - mean_one - unit * mean_two)


def split_three(vals):
    high = vals.astype(BF)
    rest = vals - high.astype(F32)
    mid = rest.astype(BF)
    low = (rest - mid.astype(F32)).astype(BF)
    return high, mid, low


def spread(flat_ref, padded_ref, images):
    for i in range(images):
        padded_ref[pl.ds(i * PAD + PAD - 16, 16), :] = jnp.zeros((16, padded_ref.shape[1]), F32)
        padded_ref[pl.ds(i * PAD, SEQ), :] = flat_ref[pl.ds(i * SEQ, SEQ), :]


def close_up(ref, images):
    for i in range(1, images):
        ref[pl.ds(i * SEQ, SEQ), :] = ref[pl.ds(i * PAD, SEQ), :]


def two_heads(pair):
    low = iota(pair.shape, 1) < HEAD_DIM
    zero = jnp.zeros_like(pair)
    gap = jnp.zeros((256 - PAD, LANES), pair.dtype)
    return jnp.concatenate([jnp.where(low, pair, zero), gap, jnp.where(low, zero, pair), gap], axis=0)


def one_pair(wide):
    merged = jnp.where(iota((LANES, 256), 0) < HEAD_DIM, wide[:, 0:256], wide[:, 256:512])
    return jnp.transpose(merged)[0:PAD]


def pair_probs(keys, q_wide):
    scores = dot_nt(keys, q_wide)
    tail = scores[PAD - 16 :]
    tail = jnp.where(iota(tail.shape, 0) < SEQ - (PAD - 16), tail, -1e30)
    scores = jnp.concatenate([scores[: PAD - 16], tail], axis=0)
    exps = jnp.exp(scores - jnp.max(scores, axis=0, keepdims=True))
    return exps * (1.0 / jnp.sum(exps, axis=0, keepdims=True))


def main_kernel(
    n_dp,
    images,
    capacity,
    x_hbm,
    cot_hbm,
    choice_ref,
    prio_ref,
    g1_ref,
    b1_ref,
    wqkv_ref,
    qvb_ref,
    wo_ref,
    ob_ref,
    g2_ref,
    b2_ref,
    wr_ref,
    win_hbm,
    ib_ref,
    wout_hbm,
    out_hbm,
    layer_hbm,
    grad_hbm,
    smallsum_ref,
    rgl_hbm,
    combl_hbm,
    qkv_hbm,
    normed_hbm,
    att_hbm,
    mid_hbm,
    xp_hbm,
    smalls_hbm,
    xs_ref,
    gp_ref,
    wts_ref,
    win_ref,
    wout_ref,
    og_ref,
    h_ref,
    dg_ref,
    comb_ref,
    rg_ref,
    gate_ref,
    acc_ref,
    sib_ref,
    landc_ref,
    landy_ref,
    landr_ref,
    landl_ref,
    fin_ref,
    gt_ref,
    gtl_ref,
    small_ref,
    sm_ref,
    dwr_ref,
    wqo_ref,
    woo_ref,
    bias_ref,
    qkvb_ref,
    bufa_ref,
    bufb_ref,
    bufc_ref,
    load_sem,
    save_sem,
    fx_sem,
    fy_sem,
    fs_sem,
    fb_sem,
    qkv_sem,
    img_sem,
    rgs_sem,
    rgr_sem,
    cs_sem,
    cr_sem,
    gt_sem,
    sib_sem,
    landc_sem,
    ys_sem,
    yr_sem,
    rs_sem,
    rr_sem,
    ls_sem,
    lr_sem,
    brs_sem,
    brr_sem,
    bls_sem,
    blr_sem,
    ars_sem,
    arr_sem,
    als_sem,
    alr_sem,
    ks_sem,
    kr_sem,
    kl_sem,
    loc_sem,
    sms_sem,
    smr_sem,
    credit_r,
    credit_l,
):
    total = images * PAD
    flat = images * SEQ
    tiles = total // 416
    nz = n_dp // 4
    deep = nz > 4
    held = acc_ref.shape[0]
    dp = lax.axis_index("dp")
    tensor = lax.axis_index("tensor")
    core = lax.rem(dp, 2)
    y = lax.rem(lax.div(dp, 2), 2)
    z = lax.div(dp, 4)
    across = {"tensor": 1 - tensor}
    sibling = {"dp": dp + 1 - 2 * core}
    ypal = {"dp": dp + 2 - 4 * y}
    right = {"dp": lax.rem(dp + 4, n_dp)}
    left = {"dp": lax.rem(dp + n_dp - 4, n_dp)}
    first, last = z == 0, z == nz - 1

    def remote(src, dst, send, recv, where):
        return pltpu.make_async_remote_copy(src, dst, send, recv, where, MESH)

    def local_copy(src, dst, sem):
        return pltpu.make_async_copy(src, dst, sem)

    flat_rows = pl.ds(0, flat)
    x_load = local_copy(x_hbm, comb_ref.at[flat_rows, :], load_sem.at[8])
    x_load.start()
    weight_loads = []
    for e in range(4):
        weight_loads.append(local_copy(win_hbm.at[e], win_ref.at[e], load_sem.at[e]))
        weight_loads.append(local_copy(wout_hbm.at[e], wout_ref.at[e], load_sem.at[4 + e]))
    barrier = pltpu.get_barrier_semaphore()
    pl.semaphore_signal(barrier, inc=1, device_id=across, device_id_type=MESH)

    @pl.loop(1, n_dp)
    def _(d):
        pl.semaphore_signal(
            barrier, inc=1, device_id={"dp": lax.rem(dp + d, n_dp)}, device_id_type=MESH
        )

    def land(j, half):
        return acc_ref.at[j, :, rows(half, 256)]

    half_rows = rows(core, 256)

    @pl.when(y == 0)
    def _():
        acc_ref[4, :, 0:256] = wqkv_ref[0, half_rows, :].astype(F32)
        acc_ref[5, :, 0:256] = wqkv_ref[2, half_rows, :].astype(F32)

    @pl.when(y == 1)
    def _():
        acc_ref[4, :, 0:256] = wqkv_ref[1, half_rows, :].astype(F32)
        acc_ref[5, :, 0:256] = wo_ref[:, half_rows].astype(F32)

    pl.semaphore_wait(barrier, n_dp)

    def fetch_x(t):
        src = acc_ref.at[4 + t, :, pl.ds(0, 256)]
        return remote(src, land(y + 2 * t, core), fx_sem.at[0, t], fx_sem.at[1, t], across)

    def fetch_y(t, mine):
        j = (y if mine else 1 - y) + 2 * t
        return remote(land(j, core), land(j, core), fy_sem.at[0, t], fy_sem.at[1, t], ypal)

    def fetch_sib(j, half):
        return remote(land(j, half), land(j, half), fs_sem.at[0, j], fs_sem.at[1, j], sibling)

    for t in range(2):
        fetch_x(t).start()
    fetch_bias = remote(qvb_ref, bias_ref, fb_sem.at[0], fb_sem.at[1], across)
    fetch_bias.start()
    for copy in weight_loads:
        copy.start()

    x_load.wait()
    spread(comb_ref, rg_ref, images)
    cot_load = local_copy(cot_hbm, comb_ref.at[flat_rows, :], load_sem.at[8])
    cot_load.start()
    xp_save = local_copy(rg_ref, xp_hbm, save_sem.at[0])
    xp_save.start()
    n_cols = pl.ds(512, 512)

    @pl.loop(0, images)
    def _(i):
        r = rows(i, PAD)
        unit, _ = norm_stats(rg_ref[r, :])
        dg_ref[3, r, n_cols] = (unit * g1_ref[...] + b1_ref[...]).astype(BF)

    normed_save = local_copy(dg_ref.at[3, :, n_cols], normed_hbm, save_sem.at[1])
    normed_save.start()

    def qkv_view(j, side):
        return (0, 0, 1)[j], (0, 512, 0)[j] + side * 256

    def project(side, weights, biases):
        @pl.loop(0, tiles)
        def _(m):
            r = rows(m, 416)
            for j in range(3):
                out = dot(dg_ref[3, r, n_cols], weights[j])
                if j == 0:
                    out = (out + biases[0:1, :]) * SCALE
                if j == 2:
                    out = out + biases[1:2, :]
                a, c = qkv_view(j, side)
                dg_ref[a, r, pl.ds(c, 256)] = out.astype(BF)

    def attend(side, start, stop):
        @pl.loop(start, stop)
        def _(i):
            r = rows(i, PAD)
            for p in range(2):
                c = side * 256 + p * LANES
                probs = pair_probs(
                    dg_ref[0, r, pl.ds(512 + c, LANES)], two_heads(dg_ref[0, r, pl.ds(c, LANES)])
                )
                wide = dot_tn(dg_ref[1, r, pl.ds(c, LANES)], probs.astype(BF))
                h_ref[r, pl.ds(c, LANES)] = one_pair(wide).astype(BF)

    project(0, wqkv_ref, qvb_ref)
    attend(0, 0, images // 2)
    for t in range(2):
        fetch_x(t).wait_recv()
        fetch_y(t, True).start()
        fetch_sib(y + 2 * t, core).start()
    attend(0, images // 2, images)
    for t in range(2):
        fetch_y(t, False).wait_recv()
        fetch_sib(1 - y + 2 * t, core).start()

    gt_ref[...] = jnp.full(gt_ref.shape, 1e6, F32)
    gt_ref[0:2, 0:flat] = choice_ref[...].astype(F32)
    gt_ref[2:3, 0:flat] = prio_ref[...].astype(F32)
    gate_ref[:, 0:8] = jnp.transpose(gt_ref[...])
    lane = iota((total, LANES), 1).astype(F32)
    hot0 = (gate_ref[:, 0:1] == lane).astype(F32)
    og_ref[:, 0:128] = hot0.astype(BF)
    og_ref[:, 128:256] = (gate_ref[:, 1:2] == lane).astype(F32).astype(BF)
    total0 = jnp.sum(hot0, axis=0, keepdims=True)

    @pl.loop(0, images)
    def _(i):
        own = gate_ref[pl.ds(i * SEQ, PAD), :]
        lane_r = iota((PAD, LANES), 1).astype(F32)
        earlier = (gt_ref[2:3, :] < own[:, 2:3]).astype(F32).astype(BF)
        pos = dot(earlier, og_ref[:, 0:256])
        kept0 = (own[:, 0:1] == lane_r) & (pos[:, 0:128] < capacity)
        kept1 = (own[:, 1:2] == lane_r) & (pos[:, 128:256] + total0 < capacity)
        real = iota((PAD, LANES), 0) < SEQ
        wts_ref[rows(i, PAD), :] = jnp.where((kept0 | kept1) & real, 1.0, 0.0)

    cot_load.wait()
    spread(comb_ref, gp_ref, images)

    wr_wide = jnp.transpose(
        jnp.concatenate([wr_ref[...], jnp.zeros((LANES - 4, wr_ref.shape[1]), F32)], axis=0)
    )
    wr_parts = split_three(wr_wide)

    fetch_bias.wait_recv()
    for j in range(4):
        fetch_sib(j, 1 - core).wait_recv()
    for j in range(3):
        wqo_ref[j, 0:256, :] = acc_ref[j, :, 0:256].astype(BF)
        wqo_ref[j, 256:512, :] = acc_ref[j, :, 256:512].astype(BF)
    woo_ref[...] = acc_ref[3].astype(BF)
    project(1, wqo_ref, bias_ref)
    qkv_saves = []
    for j in range(3):
        a, c = qkv_view(j, 0)
        qkv_saves.append(local_copy(dg_ref.at[a, :, pl.ds(c, 512)], qkv_hbm.at[j], save_sem.at[2 + j]))
        qkv_saves[-1].start()
    attend(1, 0, images)
    att_save = local_copy(h_ref.at[:, pl.ds(0, 256)], att_hbm, save_sem.at[5])
    att_save.start()

    @pl.loop(0, tiles)
    def _(m):
        r = rows(m, 416)
        branch = dot(h_ref[r, 0:256], wo_ref[...]) + dot(h_ref[r, 256:512], woo_ref[...])
        middle = rg_ref[r, :] + (branch + ob_ref[...])
        comb_ref[r, :] = middle
        unit, _ = norm_stats(middle)
        routed = (unit * g2_ref[...] + b2_ref[...]).astype(BF)
        xs_ref[r, :] = routed
        logits = dot(routed, wr_parts[0]) + dot(routed, wr_parts[1]) + dot(routed, wr_parts[2])
        logits = jnp.where(iota(logits.shape, 1) < 4, logits, -1e30)
        exps = jnp.exp(logits - jnp.max(logits, axis=1, keepdims=True))
        router = exps / jnp.sum(exps, axis=1, keepdims=True)
        kept = wts_ref[r, :]
        wts_ref[r, :] = (
            kept * router.astype(BF).astype(F32) + pltpu.roll(router, 4, 1) + pltpu.roll(kept, 8, 1)
        )

    mid_save = local_copy(comb_ref, mid_hbm, save_sem.at[6])
    mid_save.start()
    gate_ref[...] = jnp.zeros_like(gate_ref)
    small_ref[...] = jnp.zeros_like(small_ref)
    dwr_ref[...] = jnp.zeros_like(dwr_ref)
    for copy in weight_loads:
        copy.wait()
    for t in range(2):
        fetch_x(t).wait_send()
        fetch_y(t, True).wait_send()
    for j in range(4):
        fetch_sib(j, core).wait_send()
    fetch_bias.wait_send()
    for copy in [xp_save, normed_save, att_save, mid_save] + qkv_saves:
        copy.wait()
    comb_ref[...] = jnp.zeros_like(comb_ref)
    rg_ref[...] = jnp.zeros_like(rg_ref)

    def place(n, start, size):
        return out_hbm.at[n, span(core * 256 + start, size), :]

    def part(n, start, size):
        return acc_ref.at[lax.rem(n, held), span(start, size), :]

    def add(n, start, size, land_ref):
        acc_ref[lax.rem(n, held), span(start, size), :] += land_ref[...]

    def final(n, start, size):
        if deep:
            return place(n, start, size)
        return fin_ref.at[lax.rem(n, FINALS), span(start, size), :]

    def exchange_sib(n):
        slot = lax.rem(n, 2)
        return remote(
            sib_ref.at[slot], landc_ref.at[slot], sib_sem.at[slot], landc_sem.at[slot], sibling
        )

    def absorb(n):
        exchange_sib(n).wait_recv()
        acc_ref[lax.rem(n, held)] += landc_ref[lax.rem(n, 2)]

    ya = y * 128

    class Entry:
        def __init__(self, kind, v):
            self.kind = kind
            if kind == "C":
                self.there = (v >= FIRST_ATT) & (v < FIRST_ATT + 4)
                self.q = v - FIRST_ATT + 16
                self.n = 16 + lax.div(self.q - 16, 2)
                self.piece = lax.rem(self.q, 2)
                self.yrows = 64
                self.base = self.piece * 64
                self.turn = lax.rem(self.q, 2)
            else:
                self.there = (v >= 0) & (v < 16) & (lax.rem(v, 2) == (0 if kind == "A" else 1))
                self.q = v
                self.n = self.q
                self.yrows = 128
                self.base = 0
                self.turn = lax.rem(lax.div(self.q, 2), 2) + (2 if kind == "B" else 0)
            if kind == "B":
                self.right, self.left = (0, 128), (128, 128)
            else:
                size = self.yrows // 2
                self.right = (ya + self.base, size)
                self.left = (ya + self.base + size, size)

        def half(self, to_right):
            return self.right if to_right else self.left

        def y_copy(self, start):
            land_ref = landy_ref.at[self.turn, pl.ds(0, self.yrows), :]
            return remote(
                part(self.n, start, self.yrows), land_ref, ys_sem.at[self.q], yr_sem.at[self.q], ypal
            ), land_ref

        def chain_copy(self, to_right):
            start, size = self.half(to_right)
            land_ref = (landr_ref if to_right else landl_ref).at[
                lax.rem(self.q, SLOTS), pl.ds(0, size), :
            ]
            send, recv = (rs_sem, rr_sem) if to_right else (ls_sem, lr_sem)
            where = right if to_right else left
            return remote(
                part(self.n, start, size), land_ref, send.at[self.q], recv.at[self.q], where
            ), land_ref

        def spread_copy(self, src, of_right):
            send, recv = (brs_sem, brr_sem) if of_right else (bls_sem, blr_sem)
            return remote(
                src, self.spot(of_right), send.at[self.q], recv.at[self.q], left if of_right else right
            )

        def spot(self, of_right):
            return final(self.n, *self.half(of_right))

        def rows_of(self, of_right):
            return part(self.n, *self.half(of_right))

        def y_final(self, src, of_right):
            send, recv = (ars_sem, arr_sem) if of_right else (als_sem, alr_sem)
            return remote(src, self.spot(of_right), send.at[self.q], recv.at[self.q], ypal)

        def y_final_in(self, of_right):
            start, size = self.half(of_right)
            spot = final(self.n, start + 128 - 2 * ya, size)
            send, recv = (ars_sem, arr_sem) if of_right else (als_sem, alr_sem)
            return remote(spot, spot, send.at[self.q], recv.at[self.q], ypal)

        def keep(self, of_right):
            return local_copy(self.rows_of(of_right), self.spot(of_right), loc_sem.at[self.q])

    def core_final(n, half):
        return remote(
            final(n, 0, 256), out_hbm.at[n, rows(half, 256), :], ks_sem.at[n], kr_sem.at[n], sibling
        )

    def own_final(n):
        return local_copy(final(n, 0, 256), place(n, 0, 256), kl_sem.at[n])

    def at_entry(kind, v, cond, body):
        entry = Entry(kind, v)

        @pl.when(entry.there & cond)
        def _():
            body(entry)

    def finish(entry, of_right):
        src = entry.rows_of(of_right)
        if deep:
            entry.keep(of_right).start()
        else:
            start, size = entry.half(of_right)
            fin_ref[lax.rem(entry.n, FINALS), span(start, size), :] = src[...]
            src = entry.spot(of_right)
        entry.spread_copy(src, of_right).start()
        if entry.kind != "B":
            entry.y_final(src, of_right).start()

    def service(s, kinds="AB"):
        for of_right in (True, False):
            source = last if of_right else first
            sink = first if of_right else last
            v = s - nz - ((nz - 1 - z) if of_right else z)

            def passed_on(entry, of_right=of_right, sink=sink):
                here = entry.spot(of_right)
                entry.spread_copy(here, of_right).wait_recv()

                @pl.when(jnp.logical_not(sink))
                def _():
                    entry.spread_copy(here, of_right).start()

                if entry.kind != "B":
                    entry.y_final(here, of_right).start()

            for kind in kinds:
                at_entry(kind, v, jnp.logical_not(source), passed_on)

        def y_in(entry):
            copy, land_ref = entry.y_copy(128 - ya + entry.base)
            copy.wait_recv()
            add(entry.n, ya + entry.base, entry.yrows, land_ref)

        def y_out(entry):
            entry.y_copy(128 - ya + entry.base)[0].start()

        for kind in kinds:
            if kind != "B":
                at_entry(kind, s - 1, True, y_in)
        for kind in kinds:
            if kind != "B":
                at_entry(kind, s, True, y_out)

        for kind in kinds:
            for to_right in (True, False):
                hop = z if to_right else nz - 1 - z
                v = s - hop - (0 if kind == "B" else 1)
                head, end = (first, last) if to_right else (last, first)
                credit = credit_r if to_right else credit_l
                back = left if to_right else right

                def chain(entry, to_right=to_right, head=head, end=end, credit=credit, back=back):
                    copy, land_ref = entry.chain_copy(to_right)
                    start, size = entry.half(to_right)

                    @pl.when(jnp.logical_not(head))
                    def _():
                        copy.wait_recv()
                        add(entry.n, start, size, land_ref)

                        @pl.when(entry.q + SLOTS < ENTRIES)
                        def _():
                            pl.semaphore_signal(credit, inc=1, device_id=back, device_id_type=MESH)

                    @pl.when(jnp.logical_not(end))
                    def _():
                        @pl.when(entry.q >= SLOTS)
                        def _():
                            pl.semaphore_wait(credit, 1)

                        copy.start()

                    @pl.when(end)
                    def _():
                        if entry.kind == "B":
                            entry.y_copy(start)[0].start()
                        else:
                            finish(entry, to_right)

                at_entry(kind, v, True, chain)

        if "B" in kinds:
            for to_right in (True, False):

                def root(entry, to_right=to_right):
                    start, size = entry.half(to_right)
                    copy, land_ref = entry.y_copy(start)
                    copy.wait_send()
                    copy.wait_recv()
                    add(entry.n, start, size, land_ref)
                    finish(entry, to_right)

                at_entry("B", s - nz, last if to_right else first, root)

        def landed(entry):
            for of_right in (True, False):
                if entry.kind != "B":
                    entry.y_final_in(of_right).wait_recv()

                if deep:

                    @pl.when(last if of_right else first)
                    def _():
                        entry.keep(of_right).wait()

            def whole():
                core_final(entry.n, core).start()
                if not deep:
                    own_final(entry.n).start()

            if entry.kind == "C":
                pl.when(entry.piece == 1)(whole)
            else:
                whole()

        def from_sibling(entry):
            def whole():
                core_final(entry.n, 1 - core).wait_recv()
                core_final(entry.n, core).wait_send()
                if not deep:
                    own_final(entry.n).wait()

            for to_right in (True, False):
                end = last if to_right else first
                head = first if to_right else last

                @pl.when(jnp.logical_not(end))
                def _():
                    entry.chain_copy(to_right)[0].wait_send()

                @pl.when(jnp.logical_not(head))
                def _():
                    entry.spread_copy(entry.rows_of(to_right), to_right).wait_send()

                if entry.kind != "B":
                    entry.y_final(entry.rows_of(to_right), to_right).wait_send()
            if entry.kind != "B":
                entry.y_copy(128 - ya + entry.base)[0].wait_send()
            if entry.kind == "C":
                pl.when(entry.piece == 1)(whole)
            else:
                whole()

        for kind in kinds:
            at_entry(kind, s - 2 * nz, True, landed)
        for kind in kinds:
            at_entry(kind, s - (2 * nz + 1), True, from_sibling)

    @pl.loop(0, 8)
    def _(u):
        e = lax.div(u, 2)
        f = lax.rem(u, 2)
        chunk = rows(f, 512)

        @pl.when(f == 0)
        def _():
            @pl.loop(0, images)
            def _(i):
                r = rows(i, PAD)
                og_ref[r, :] = (column(wts_ref[r, :], e) * gp_ref[r, :]).astype(BF)

        def inner(m):
            r = pl.ds(m * 416, 416)
            for c in range(2):
                cols = pl.ds(pl.multiple_of(f * 512 + c * 256, 256), 256)
                pre = dot(xs_ref[r, :], win_ref[e, :, cols]) + ib_ref[pl.ds(e, 1), cols]
                sq = pre * pre
                arg = pre * (0.7978845608028654 + 0.035677408136300125 * sq)
                th = jnp.tanh(arg)
                half = 0.5 + 0.5 * th
                act = pre * half
                h_ref[r, pl.ds(c * 256, 256)] = act.astype(BF)
                slope = 1.5957691216057308 + 0.21406444881780074 * sq
                dg_ref[e, r, cols] = (half + act * (1.0 - half) * slope).astype(BF)

        def outer(m):
            r = pl.ds(m * 416, 416)
            eo = dot(h_ref[r, :], wout_ref[e, chunk, :])
            comb_ref[r, :] += column(wts_ref[r, :], e) * eo
            product = jnp.sum(gp_ref[r, :] * eo, axis=1, keepdims=True)
            gate_ref[r, :] += jnp.where(iota((416, LANES), 1) == e, product, 0.0)

        inner(0)
        for m in range(1, tiles):
            inner(m)
            outer(m - 1)
        outer(tiles - 1)

        @pl.when(u >= 2)
        def _():
            exchange_sib(u - 2).wait_send()

        sib_ref[lax.rem(u, 2)] = dot_tn(h_ref[:, rows(1 - core, 256)], og_ref[...])

        @pl.when(u >= 1)
        def _():
            absorb(u - 1)

        exchange_sib(u).start()
        acc_ref[lax.rem(u, held)] = dot_tn(h_ref[:, rows(core, 256)], og_ref[...])

        @pl.when(f == 1)
        def _():
            service(e)

    gt_ref[...] = jnp.transpose(gate_ref[...])[0:8, :]
    gt_copy = remote(gt_ref, gtl_ref, gt_sem.at[0], gt_sem.at[1], across)
    gt_copy.start()

    def comb_copy(i):
        r = pl.ds(pl.multiple_of(i * PAD, PAD), SENT)
        return remote(comb_ref.at[r, :], combl_hbm.at[r, :], cs_sem.at[i], cr_sem.at[i], across)

    def rg_copy(i):
        r = pl.ds(pl.multiple_of(i * PAD, PAD), SENT)
        return remote(rg_ref.at[r, :], rgl_hbm.at[r, :], rgs_sem.at[i], rgr_sem.at[i], across)

    @pl.loop(0, tiles)
    def _(m):
        r = rows(m, 416)

        @pl.loop(0, 4)
        def _(e):
            og_ref[r, :] = (column(wts_ref[r, :], e) * gp_ref[r, :]).astype(BF)
            for c in range(4):
                cols = pl.ds(c * 256, 256)
                hg = dot_nt(og_ref[r, :], wout_ref[e, cols, :])
                pg = (hg * dg_ref[e, r, cols].astype(F32)).astype(BF)
                dg_ref[e, r, cols] = pg
                at = pl.ds(6 + 2 * e + c // 2, 1)
                small_ref[at, pl.ds((c % 2) * 256, 256)] += jnp.sum(
                    pg.astype(F32), axis=0, keepdims=True
                )
            rg_ref[r, :] += dot_nt(dg_ref[e, r, :], win_ref[e])

        rg_copy(2 * m).start()
        rg_copy(2 * m + 1).start()

        @pl.when(m == 0)
        def _():
            absorb(7)

        service(4 + m)

    def qkv_load(i, j):
        return local_copy(
            qkv_hbm.at[j, rows(i, PAD), :], qkvb_ref.at[lax.rem(i, 2), j], qkv_sem.at[lax.rem(i, 2), j]
        )

    def side_load(i, src, cols, k):
        dst = win_ref.at[lax.div(i, 2), rows(lax.rem(i, 2), PAD), cols]
        return local_copy(src.at[rows(i, PAD), :], dst, load_sem.at[k])

    for j in range(3):
        qkv_load(0, j).start()
    gt_copy.wait_recv()
    gt_copy.wait_send()
    gate_ref[...] = jnp.transpose(
        jnp.concatenate([gt_ref[...] + gtl_ref[...], jnp.zeros((LANES - 8, total), F32)], axis=0)
    )

    @pl.loop(0, images)
    def _(i):
        r = rows(i, PAD)
        fetch = [
            local_copy(mid_hbm.at[r, :], bufa_ref, img_sem.at[0]),
            local_copy(xp_hbm.at[r, :], bufb_ref, img_sem.at[1]),
            side_load(i, normed_hbm, pl.ds(256, 512), 0),
            side_load(i, att_hbm, pl.ds(768, 256), 1),
        ]
        for copy in fetch:
            copy.start()

        @pl.when(i >= images // 2)
        def _():
            for k in range(2):
                comb_copy(2 * i - images + k).start()

        @pl.when(i + 1 < images)
        def _():
            for j in range(3):
                qkv_load(i + 1, j).start()

        e = lax.div(i, 2)
        f = lax.rem(i, 2)
        n = 8 + i

        exchange_sib(n - 2).wait_send()
        sib_ref[lax.rem(n, 2)] = dot_tn(xs_ref[:, rows(1 - core, 256)], dg_ref[e, :, rows(f, 512)])
        exchange_sib(n).start()
        acc_ref[lax.rem(n, held)] = dot_tn(xs_ref[:, rows(core, 256)], dg_ref[e, :, rows(f, 512)])
        rg_copy(i).wait_recv()
        late = local_copy(rgl_hbm.at[r, :], bufc_ref, img_sem.at[4])
        late.start()
        for copy in fetch:
            copy.wait()
        for j in range(3):
            qkv_load(i, j).wait()
        packed = wts_ref[r, :]
        low4 = iota(packed.shape, 1) < 4
        router = jnp.where(low4, pltpu.roll(packed, LANES - 4, 1), 0.0)
        kept = jnp.where(low4, pltpu.roll(packed, LANES - 8, 1), 0.0)
        gg = kept * gate_ref[r, :]
        dl = router * (gg - jnp.sum(router * gg, axis=1, keepdims=True))
        unit, inv = norm_stats(bufa_ref[...])
        late.wait()
        real = iota((PAD, 512), 0) < SEQ
        grad = jnp.where(real, rg_ref[r, :] + bufc_ref[...], 0.0)
        for k in range(4):
            grad = grad + dl[:, k : k + 1] * wr_ref[k : k + 1, :]
        routed = xs_ref[r, :]
        for piece in split_three(dl):
            dwr_ref[...] += dot_tn(piece, routed)
        small_ref[2:3, :] += jnp.sum(grad * unit, axis=0, keepdims=True)
        small_ref[3:4, :] += jnp.sum(grad, axis=0, keepdims=True)
        middle_grad = gp_ref[r, :] + norm_back(grad, g2_ref[...], unit, inv)
        bufa_ref[...] = middle_grad
        branch = middle_grad.astype(BF)
        og_ref[r, :] = branch
        small_ref[4:5, :] += jnp.sum(branch.astype(F32), axis=0, keepdims=True)
        slot = lax.rem(i, 2)
        four = lax.div(i, 4)
        four_rows = rows(lax.rem(i, 4), PAD)
        two_rows = rows(lax.rem(i, 2), PAD)
        for p in range(4):
            cols = pl.ds(p * LANES, LANES)
            weights = (wo_ref if p < 2 else woo_ref)[pl.ds((p % 2) * LANES, LANES), :]
            a_wide = two_heads(dot_nt(branch, weights).astype(BF))
            keys = qkvb_ref[slot, 1, :, cols]
            q_wide = two_heads(qkvb_ref[slot, 0, :, cols])
            probs = pair_probs(keys, q_wide)
            dv = dot(probs.astype(BF), a_wide).astype(BF)
            dpr = dot_nt(qkvb_ref[slot, 2, :, cols], a_wide)
            ds = (probs * (dpr - jnp.sum(dpr * probs, axis=0, keepdims=True))).astype(BF)
            dk = dot(ds, q_wide).astype(BF)
            dq = (one_pair(dot_tn(keys, ds)) * SCALE).astype(BF)
            wout_ref[2, pl.ds(0, PAD), cols] = dq
            wout_ref[2, pl.ds(PAD, PAD), cols] = dk
            wout_ref[2, pl.ds(2 * PAD, PAD), cols] = dv
            if p < 2:
                wout_ref[four, four_rows, cols] = dq
                wout_ref[four, four_rows, pl.ds(256 + p * LANES, LANES)] = dk
                win_ref[lax.div(i, 2), two_rows, cols] = dv
        absorb(n)
        service(n)
        ngrad = jnp.zeros((PAD, 512), F32)
        for j in range(3):
            d = wout_ref[2, pl.ds(j * PAD, PAD), :]
            ngrad += dot_nt(d[:, 0:256], wqkv_ref[j]) + dot_nt(d[:, 256:512], wqo_ref[j])
        q_own = wout_ref[2, pl.ds(0, PAD), 0:256].astype(F32)
        v_own = wout_ref[2, pl.ds(2 * PAD, PAD), 0:256].astype(F32)
        small_ref[5:6, 0:256] += jnp.sum(q_own, axis=0, keepdims=True)
        small_ref[5:6, 256:512] += jnp.sum(v_own, axis=0, keepdims=True)
        unit, inv = norm_stats(bufb_ref[...])
        small_ref[0:1, :] += jnp.sum(ngrad * unit, axis=0, keepdims=True)
        small_ref[1:2, :] += jnp.sum(ngrad, axis=0, keepdims=True)
        result = bufa_ref[...] + norm_back(ngrad, g1_ref[...], unit, inv)
        gp_ref[r, :] = result

    @pl.loop(0, images)
    def _(i):
        rg_copy(i).wait_send()

    close_up(gp_ref, images)
    grad_save = local_copy(gp_ref.at[flat_rows, :], grad_hbm, save_sem.at[0])
    grad_save.start()
    small_ref[14:18, :] = dwr_ref[0:4, :]

    def small_copy(d):
        return remote(
            small_ref,
            smalls_hbm.at[dp],
            sms_sem.at[d],
            smr_sem.at[d],
            {"dp": lax.rem(dp + d, n_dp)},
        )

    small_own = local_copy(small_ref, smalls_hbm.at[dp], sms_sem.at[0])
    small_own.start()

    @pl.loop(1, n_dp)
    def _(d):
        small_copy(d).start()

    def over_images(left_of, right_of):
        return sum(dot_tn(left_of(b), right_of(b)) for b in range(images // 2))

    def normed_of(c):
        cols = pl.ds(pl.multiple_of(256 + c * 256, 256), 256)
        return lambda b: win_ref[b, pl.ds(0, 416), cols]

    def qk_of(k):
        return lambda b: wout_ref[b // 2, pl.ds((b % 2) * 416, 416), pl.ds(k * 256, 256)]

    def query_key(c, dst):
        dst[:, 0:256] = over_images(normed_of(c), qk_of(0))
        dst[:, 256:512] = over_images(normed_of(c), qk_of(1))

    def value_out(c, dst):
        dst[:, 0:256] = over_images(normed_of(c), lambda b: win_ref[b, pl.ds(0, 416), pl.ds(0, 256)])
        dst[:, 256:512] = over_images(
            lambda b: win_ref[b, pl.ds(0, 416), pl.ds(768, 256)],
            lambda b: og_ref[pl.ds(b * 416, 416), rows(c, 256)],
        )

    for n, fill in ((16, query_key), (17, value_out)):
        exchange_sib(n - 2).wait_send()
        fill(1 - core, sib_ref.at[n % 2])
        exchange_sib(n).start()
        fill(core, acc_ref.at[n % held])
        absorb(n)
        if n == 16:
            service(16, "ABC")
            service(17, "ABC")

    @pl.loop(0, images)
    def _(i):
        r = rows(i, PAD)
        service(18 + i, "ABC")
        comb_copy(i).wait_recv()
        fetch = [
            local_copy(mid_hbm.at[r, :], bufa_ref, img_sem.at[0]),
            local_copy(combl_hbm.at[r, :], bufb_ref, img_sem.at[1]),
        ]
        for copy in fetch:
            copy.start()
        comb_copy(i).wait_send()
        for copy in fetch:
            copy.wait()
        result = bufa_ref[...] + (comb_ref[r, :] + bufb_ref[...])
        comb_ref[r, :] = result

    close_up(comb_ref, images)
    layer_save = local_copy(comb_ref.at[flat_rows, :], layer_hbm, save_sem.at[1])
    layer_save.start()

    smallsum_ref[...] = jnp.zeros_like(smallsum_ref)
    small_own.wait()

    @pl.loop(1, n_dp)
    def _(d):
        source = lax.rem(dp + n_dp - d, n_dp)
        remote(small_ref, smalls_hbm.at[source], sms_sem.at[d], smr_sem.at[d], sibling).wait_recv()

    @pl.loop(0, n_dp // 16)
    def _(g):
        copy = local_copy(smalls_hbm.at[rows(g, 16)], sm_ref, img_sem.at[2])
        copy.start()
        copy.wait()

        @pl.loop(0, 16)
        def _(d):
            smallsum_ref[...] += sm_ref[d]

    @pl.loop(18 + images, FIRST_ATT + 3 + 2 * nz + 2)
    def _(s):
        service(s, "ABC")

    @pl.loop(1, n_dp)
    def _(d):
        small_copy(d).wait_send()

    for n in (16, 17):
        exchange_sib(n).wait_send()

    grad_save.wait()
    layer_save.wait()


def finish_kernel(
    units_hbm,
    layer_in,
    grad_in,
    small_ref,
    layer_out,
    grad_out,
    g1_ref,
    b1_ref,
    dwqkv_hbm,
    qvb_ref,
    dwo_hbm,
    ob_ref,
    g2_ref,
    b2_ref,
    dwr_ref,
    dwin_hbm,
    dib_ref,
    dwout_hbm,
    sem,
    *stages,
):
    pairs = []
    for e in range(4):
        for f in range(2):
            chunk = pl.ds(f * 512, 512)
            pairs.append((units_hbm.at[2 * e + f], dwout_hbm.at[e, chunk, :]))
            pairs.append((units_hbm.at[8 + 2 * e + f], dwin_hbm.at[e, :, chunk]))
    low, high = pl.ds(0, 256), pl.ds(256, 256)
    pairs += [
        (units_hbm.at[16, :, low], dwqkv_hbm.at[0]),
        (units_hbm.at[16, :, high], dwqkv_hbm.at[1]),
        (units_hbm.at[17, :, low], dwqkv_hbm.at[2]),
        (units_hbm.at[17, low, high], dwo_hbm.at[:, low]),
        (units_hbm.at[17, high, high], dwo_hbm.at[:, high]),
        (layer_in, layer_out),
        (grad_in, grad_out),
    ]
    ins = [
        pltpu.make_async_copy(src, stages[k], sem.at[0, k]) for k, (src, _) in enumerate(pairs)
    ]
    results = [
        pltpu.make_async_copy(stages[k], dst, sem.at[1, k]) for k, (_, dst) in enumerate(pairs)
    ]
    for copy in ins:
        copy.start()
    g1_ref[...] = small_ref[0:1, :]
    b1_ref[...] = small_ref[1:2, :]
    g2_ref[...] = small_ref[2:3, :]
    b2_ref[...] = small_ref[3:4, :]
    ob_ref[...] = small_ref[4:5, :]
    qvb_ref[0:1, :] = small_ref[5:6, 0:256]
    qvb_ref[1:2, :] = small_ref[5:6, 256:512]
    for e in range(4):
        for f in range(2):
            k = 6 + 2 * e + f
            dib_ref[e : e + 1, pl.ds(f * 512, 512)] = small_ref[k : k + 1, :]
    dwr_ref[...] = small_ref[14:18, :]
    for copy_in, copy_out in zip(ins, results):
        copy_in.wait()
        copy_out.start()
    for copy in results:
        copy.wait()


def local(
    layer_input,
    cotangent,
    ln1_gain,
    ln1_shift,
    w_qkv,
    qv_bias,
    w_out,
    out_bias,
    ln2_gain,
    ln2_shift,
    w_router,
    w_in,
    in_bias,
    w_hidden_out,
    choices,
    priority,
    *,
    n_dp,
):
    tokens, width = layer_input.shape
    experts = w_in.shape[0]
    capacity = (5 * tokens + 2 * experts - 1) // (2 * experts)
    images = tokens // SEQ
    total = images * PAD
    sds = jax.ShapeDtypeStruct
    vmem = pl.BlockSpec(memory_space=pltpu.VMEM)
    hbm = pl.BlockSpec(memory_space=pl.ANY)
    row = lambda v: v.reshape(1, -1)
    dma = pltpu.SemaphoreType.DMA
    block = (128, width)
    outs = pl.pallas_call(
        functools.partial(main_kernel, n_dp, images, capacity),
        out_shape=(
            sds((UNITS, 512, 512), F32),
            sds((tokens, width), F32),
            sds((tokens, width), F32),
            sds((SMALL, width), F32),
            sds((total, width), F32),
            sds((total, width), F32),
            sds((3, total, width), BF),
            sds((total, width), BF),
            sds((total, 256), BF),
            sds((total, width), F32),
            sds((total, width), F32),
            sds((n_dp, SMALL, width), F32),
        ),
        in_specs=[hbm, hbm] + [vmem] * 11 + [hbm, vmem, hbm],
        out_specs=(hbm, hbm, hbm, vmem) + (hbm,) * 8,
        scratch_shapes=[
            pltpu.VMEM((total, width), BF),
            pltpu.VMEM((total, width), F32),
            pltpu.VMEM((total, LANES), F32),
            pltpu.VMEM(w_in.shape, BF),
            pltpu.VMEM(w_hidden_out.shape, BF),
            pltpu.VMEM((total, width), BF),
            pltpu.VMEM((total, width), BF),
            pltpu.VMEM((experts, total, 1024), BF),
            pltpu.VMEM((total, width), F32),
            pltpu.VMEM((total, width), F32),
            pltpu.VMEM((total, LANES), F32),
            pltpu.VMEM((12 if n_dp <= 16 else UNITS, 256, width), F32),
            pltpu.VMEM((2, 256, width), F32),
            pltpu.VMEM((2, 256, width), F32),
            pltpu.VMEM((4,) + block, F32),
            pltpu.VMEM((SLOTS,) + block, F32),
            pltpu.VMEM((SLOTS,) + block, F32),
            pltpu.VMEM((FINALS if n_dp <= 16 else 1, 256, width), F32),
            pltpu.VMEM((8, total), F32),
            pltpu.VMEM((8, total), F32),
            pltpu.VMEM((SMALL, width), F32),
            pltpu.VMEM((16, SMALL, width), F32),
            pltpu.VMEM((LANES, width), F32),
            pltpu.VMEM(w_qkv.shape, BF),
            pltpu.VMEM(w_out.shape, BF),
            pltpu.VMEM(qv_bias.shape, F32),
            pltpu.VMEM((2, 3, PAD, width), BF),
            pltpu.VMEM((PAD, width), F32),
            pltpu.VMEM((PAD, width), F32),
            pltpu.VMEM((PAD, width), F32),
            dma((9,)),
            dma((7,)),
            dma((2, 2)),
            dma((2, 2)),
            dma((2, 4)),
            dma((2,)),
            dma((2, 3)),
            dma((5,)),
            dma((images,)),
            dma((images,)),
            dma((images,)),
            dma((images,)),
            dma((2,)),
            dma((2,)),
            dma((2,)),
        ]
        + [dma((ENTRIES,)) for _ in range(14)]
        + [dma((UNITS,)), dma((UNITS,)), dma((UNITS,)), dma((ENTRIES,))]
        + [
            dma((n_dp,)),
            dma((n_dp,)),
            pltpu.SemaphoreType.REGULAR,
            pltpu.SemaphoreType.REGULAR,
        ],
        compiler_params=pltpu.CompilerParams(
            collective_id=1, has_side_effects=True, vmem_limit_bytes=63 * MIB
        ),
        name="layer",
    )(
        layer_input,
        cotangent,
        choices.T,
        priority,
        row(ln1_gain),
        row(ln1_shift),
        w_qkv,
        qv_bias,
        w_out,
        row(out_bias),
        row(ln2_gain),
        row(ln2_shift),
        w_router.T,
        w_in,
        in_bias,
        w_hidden_out,
    )
    units, layer_out, input_grad, small = outs[:4]
    vector = sds((1, width), F32)
    results = pl.pallas_call(
        finish_kernel,
        out_shape=(
            sds(layer_input.shape, F32),
            sds(layer_input.shape, F32),
            vector,
            vector,
            sds(w_qkv.shape, F32),
            sds(qv_bias.shape, F32),
            sds(w_out.shape, F32),
            vector,
            vector,
            vector,
            sds(w_router.shape[::-1], F32),
            sds(w_in.shape, F32),
            sds(in_bias.shape, F32),
            sds(w_hidden_out.shape, F32),
        ),
        in_specs=[hbm, hbm, hbm, vmem],
        out_specs=(hbm, hbm, vmem, vmem, hbm, vmem, hbm, vmem, vmem, vmem, vmem, hbm, vmem, hbm),
        scratch_shapes=[dma((2, 23))]
        + [pltpu.VMEM((512, 512), F32)] * 16
        + [pltpu.VMEM((512, 256), F32)] * 3
        + [pltpu.VMEM((256, 256), F32)] * 2
        + [pltpu.VMEM((tokens, width), F32)] * 2,
        compiler_params=pltpu.CompilerParams(vmem_limit_bytes=62 * MIB),
        name="finish",
    )(units, layer_out, input_grad, small)
    results = [v.reshape(width) if v.shape == (1, width) else v for v in results]
    results[10] = results[10].T
    return tuple(results)


def solution(mesh):
    whole = P()
    placed = (
        P("dp", None),
        P("dp", None),
        whole,
        whole,
        P(None, None, "tensor"),
        P(None, "tensor"),
        P("tensor", None),
        whole,
        whole,
        whole,
        whole,
        P(None, None, "tensor"),
        P(None, "tensor"),
        P(None, "tensor", None),
        P("dp", None),
        P("dp", None),
    )
    grads = placed[2:14]
    return jax.shard_map(
        functools.partial(local, n_dp=mesh.shape["dp"]),
        mesh=mesh,
        in_specs=placed,
        out_specs=(P("dp", None), P("dp", None)) + grads,
        check_vma=False,
    )
```

time: 975 us -> 334 us (0.34)
  waiting for transfers between devices: 413 us -> 0 us
  Pallas kernels: 0 us -> 332 us
  local copies, waits for them, and re-layouts: 279 us -> 0 us
  matrix products: 125 us -> 0 us
  other arithmetic: 68.6 us -> 0 us
  blocking collectives: 68.2 us -> 0 us
  between operations: 15.1 us -> 0.84 us
    psum x4 -> x0, waiting for transfers between devices: 413 us -> none  [the longest x1 263 us: local(): lax.psum((ln1_gain_grad, ln1_shift_grad, w_qkv_grad, qv_bias_grad, w_out_...]
    pallas_call x0 -> x2, Pallas kernels: none -> 332 us  [the longest x1 313 us: local(): pl.pallas_call(functools.partial(main_kernel, n_dp, images, capacity), ou...]
    dot_general x21 -> x0, matrix products: 125 us -> none  [the longest x1 19.6 us: local(): jnp.einsum('ecd,efd->ecf', out_grad, w_hidden_out, preferred_element_type...]
    gather x17 -> x0, local copies, waits for them, and re-layouts: 121 us -> none  [the longest x7 40.4 us: route(): return jnp.take_along_axis(router, choices, axis=1)]
    psum x2 -> x0, blocking collectives: 68.2 us -> none  [the longest x1 60.7 us: local(): lax.psum((ln1_gain_grad, ln1_shift_grad, w_qkv_grad, qv_bias_grad, w_out_...]
    scatter x3 -> x0, local copies, waits for them, and re-layouts: 40.7 us -> none  [the longest x1 15.8 us: slot_table(): slot_token = jnp.full((experts_n * capacity + 1,), tok_count, jnp.int32)....]
    unnamed x156 -> x0, local copies, waits for them, and re-layouts: 28.9 us -> none
    reshape x11 -> x0, local copies, waits for them, and re-layouts: 27.1 us -> none  [the longest x1 7.65 us: local(): partial_out.reshape(experts_n * capacity, model_width)]
  transfers between devices with their start and end apart: 4 -> 0, of which waited for: 4 -> 0; matrix products, arithmetic and copies ran while one was open for 19% -> 0% of each run, Pallas kernels for 0% -> 0%
where the time goes in v1:
time: 334 us; the launch traced here: 333 us
  Pallas kernels  332 us (99%)
    pallas_call x1, Pallas kernels, local(): pl.pallas_call(functools.partial(main_kernel, n_dp, images, capacity), ou...  313 us
    pallas_call x1, Pallas kernels, local(): pl.pallas_call(finish_kernel, out_shape=(sds(layer_input.shape, F32), sds...  18.7 us

profile of v1, /device:TPU:3, one launch (start us, length us, event | category | flops | bytes accessed | tf_op | source)
XLA Modules:
  0.0 332.9 jit_solution(13274202260203218258)
XLA Ops:
  0.7 313.3 %layer.1 = (f32[18,512,512]{2,1,0:T(8,128)}, f32[1576,512]{1,0:T(8,128)}, f32[1576,512]{1,0:T(8,128)}, f32[24,512]{1,0:T(8,128)}, f32[1664,512]{1,0:T(8,128)}, /...) custom-call(f32[1576,512]{1,0:T(8,128)} %x_hbm.1, ...), custom_call_target="tpu_custom_call" | custom-call | tf_op jit(solution)/shard_map/layer/pallas_call | solution.py:1104
  314.0 18.7 %finish.1 = (f32[1576,512]{1,0:T(8,128)}, f32[1576,512]{1,0:T(8,128)}, f32[1,512]{1,0:T(1,128)}, f32[1,512]{1,0:T(1,128)}, f32[3,512,256]{2,1,0:T(8,128)}, /*ind...) custom-call(f32[18,512,512]{2,1,0:T(8,128)} %get-tuple-element.32.un, ...), custom_call_target="tpu_custom_call" | custom-call | tf_op jit(solution)/shard_map/finish/pallas_call | solution.py:1201

commit v2 on v1

--- a/solution.py
+++ b/solution.py
@@ -424,11 +424,14 @@
     def place(n, start, size):
         return out_hbm.at[n, span(core * 256 + start, size), :]
 
+    def slot_of(n):
+        return n - jnp.where(n >= held, held, 0)
+
     def part(n, start, size):
-        return acc_ref.at[lax.rem(n, held), span(start, size), :]
+        return acc_ref.at[slot_of(n), span(start, size), :]
 
     def add(n, start, size, land_ref):
-        acc_ref[lax.rem(n, held), span(start, size), :] += land_ref[...]
+        acc_ref[slot_of(n), span(start, size), :] += land_ref[...]
 
     def final(n, start, size):
         if deep:
@@ -443,7 +446,7 @@
 
     def absorb(n):
         exchange_sib(n).wait_recv()
-        acc_ref[lax.rem(n, held)] += landc_ref[lax.rem(n, 2)]
+        acc_ref[slot_of(n)] += landc_ref[lax.rem(n, 2)]
 
     ya = y * 128
 
@@ -735,7 +738,7 @@
             absorb(u - 1)
 
         exchange_sib(u).start()
-        acc_ref[lax.rem(u, held)] = dot_tn(h_ref[:, rows(core, 256)], og_ref[...])
+        acc_ref[slot_of(u)] = dot_tn(h_ref[:, rows(core, 256)], og_ref[...])
 
         @pl.when(f == 1)
         def _():
@@ -826,7 +829,7 @@
         exchange_sib(n - 2).wait_send()
         sib_ref[lax.rem(n, 2)] = dot_tn(xs_ref[:, rows(1 - core, 256)], dg_ref[e, :, rows(f, 512)])
         exchange_sib(n).start()
-        acc_ref[lax.rem(n, held)] = dot_tn(xs_ref[:, rows(core, 256)], dg_ref[e, :, rows(f, 512)])
+        acc_ref[slot_of(n)] = dot_tn(xs_ref[:, rows(core, 256)], dg_ref[e, :, rows(f, 512)])
         rg_copy(i).wait_recv()
         late = local_copy(rgl_hbm.at[r, :], bufc_ref, img_sem.at[4])
         late.start()

time: 334 us -> 334 us (level)
  no operation moved by 1% of the time
where the time goes in v2:
time: 334 us; the launch traced here: 333 us
  Pallas kernels  332 us (99%)
    pallas_call x1, Pallas kernels, local(): pl.pallas_call(functools.partial(main_kernel, n_dp, images, capacity), ou...  313 us
    pallas_call x1, Pallas kernels, local(): pl.pallas_call(finish_kernel, out_shape=(sds(layer_input.shape, F32), sds...  18.7 us

profile of v2, /device:TPU:3, one launch (start us, length us, event | category | flops | bytes accessed | tf_op | source)
XLA Modules:
  0.0 332.9 jit_solution(12123846572866422032)
XLA Ops:
  0.7 313.3 %layer.1 = (f32[18,512,512]{2,1,0:T(8,128)}, f32[1576,512]{1,0:T(8,128)}, f32[1576,512]{1,0:T(8,128)}, f32[24,512]{1,0:T(8,128)}, f32[1664,512]{1,0:T(8,128)}, /...) custom-call(f32[1576,512]{1,0:T(8,128)} %x_hbm.1, ...), custom_call_target="tpu_custom_call" | custom-call | tf_op jit(solution)/shard_map/layer/pallas_call | solution.py:1107
  313.9 18.7 %finish.1 = (f32[1576,512]{1,0:T(8,128)}, f32[1576,512]{1,0:T(8,128)}, f32[1,512]{1,0:T(1,128)}, f32[1,512]{1,0:T(1,128)}, f32[3,512,256]{2,1,0:T(8,128)}, /*ind...) custom-call(f32[18,512,512]{2,1,0:T(8,128)} %get-tuple-element.32.un, ...), custom_call_target="tpu_custom_call" | custom-call | tf_op jit(solution)/shard_map/finish/pallas_call | solution.py:1204
